TPU v7x, 32 devices: a whole 2x2x4 slice. The times are simulated.
32 devices in a mesh: freq: 8 (over z, x), bl: 4 (over y, core).
Axes of the slice: x: 2, y: 2, z: 4, core: 2. Of those that a mesh axis runs over, the one named last changes fastest.
Arguments:
- vis_time: bfloat16 [8, 2, 1024, 2048], P('freq', None, 'bl'), may hold values from -6 to 6
- owner: int32 [24, 1], replicated, may hold values from 0 to 7; in each aligned block of 24 rows (0 to 23, 24 to 47, ...) at most 4 rows name the same one
- counts: int32 [24, 8], replicated, may hold values from 1 to 4
- factors: bfloat16 [32, 8, 2, 4, 1024], P('freq', None, None, None, 'bl'), may hold values from -0.1875 to 0.1875
Outputs:
- filtered: bfloat16 [8, 2, 1024, 24], P('freq', None, 'bl')
Inputs may be any that keep to these rules, and one draw needn't show every extreme that they name: `owner`: every index of freq owns at least one m and at most 4; some index owns exactly 4.
All inputs are finite; a program needn't handle non-finite values.
Results may differ from a plain program's by a relative error of at most 0.0064.
Values may be sent and summed in bfloat16 or wider, within the bound.
A program may use at most 64 MiB of HBM per device.

v0:
```python
import math

import jax
import jax.numpy as jnp
from jax import lax
from jax.sharding import PartitionSpec as P

NB = 1024
K = 4


def wave_tables(columns, samples):
    times = jnp.arange(samples, dtype=jnp.int32)
    phases = times[:, None] * columns[None, :] % samples
    angles = phases.astype(jnp.float32) * (2.0 * math.pi / samples)
    factor_scale = 1.0 / math.sqrt(samples)
    return jnp.concatenate(
        [jnp.cos(angles) * factor_scale, jnp.sin(angles) * factor_scale], axis=1
    ).astype(jnp.bfloat16)


def spectrum(flattened, wave_table, freq_here, base_here):
    width = wave_table.shape[1] // 2
    spectra = jnp.dot(flattened, wave_table, preferred_element_type=jnp.float32).reshape(
        freq_here, 2, base_here, 2, width
    )
    real_part = spectra[:, 0, :, 0] + spectra[:, 1, :, 1]
    imag_part = spectra[:, 1, :, 0] - spectra[:, 0, :, 1]
    return jnp.stack([real_part, imag_part], axis=1).astype(jnp.bfloat16)


def mask_round(coef, limits):
    rank_ids = jnp.arange(coef.shape[3], dtype=jnp.int32)
    retained = rank_ids[None, None, None, :] < limits[:, :, None, None]
    return jnp.where(retained, coef, 0.0).astype(jnp.bfloat16)


def local(vis_time, owner, counts, factors):
    n_freq = lax.axis_size("freq")
    myself = lax.axis_index("freq")
    freq_here, _, base_here, samples = vis_time.shape
    mode_count = owner.shape[0]
    capacity = factors.shape[0]
    slot_total = capacity * n_freq
    owners_of = owner[:, 0]
    owner_ids = jnp.arange(n_freq, dtype=jnp.int32)
    onehot = (owners_of[:, None] == owner_ids[None, :]).astype(jnp.int32)
    before = jnp.cumsum(onehot, axis=0) - onehot
    ranking = jnp.sum(before * onehot, axis=1)
    slot_of = owners_of * capacity + ranking
    mode_ids = jnp.arange(mode_count, dtype=jnp.int32)
    placing = slot_of[None, :] == jnp.arange(slot_total, dtype=jnp.int32)[:, None]
    placing_bf = placing.astype(jnp.bfloat16)
    flattened = vis_time.reshape(freq_here * 2 * base_here, samples)
    m_modes = spectrum(flattened, wave_tables(mode_ids, samples), freq_here, base_here)
    outgoing = jnp.einsum(
        "sm,fpbm->fspb", placing_bf, m_modes, preferred_element_type=jnp.float32
    ).astype(jnp.bfloat16)
    incoming = lax.all_to_all(outgoing, "freq", split_axis=1, concat_axis=0, tiled=True)
    mine = lax.dynamic_slice_in_dim(placing.astype(jnp.int32), myself * capacity, capacity, 0)
    limits = jnp.dot(mine, counts)
    fac_re = factors[:, :, 0]
    fac_im = factors[:, :, 1]
    vis_re = incoming[:, :, 0]
    vis_im = incoming[:, :, 1]
    coef_re = jnp.einsum(
        "cfkb,fcb->cfk", fac_re, vis_re, preferred_element_type=jnp.float32
    ) + jnp.einsum("cfkb,fcb->cfk", fac_im, vis_im, preferred_element_type=jnp.float32)
    coef_im = jnp.einsum(
        "cfkb,fcb->cfk", fac_re, vis_im, preferred_element_type=jnp.float32
    ) - jnp.einsum("cfkb,fcb->cfk", fac_im, vis_re, preferred_element_type=jnp.float32)
    partial_coef = jnp.stack([coef_re, coef_im], axis=2)
    summed = lax.psum(partial_coef, "bl")
    kept = mask_round(summed, limits)
    kept_re = kept[:, :, 0]
    kept_im = kept[:, :, 1]
    factor_scale = math.sqrt(NB / K)
    syn_re = (
        jnp.einsum("cfkb,cfk->fcb", fac_re, kept_re, preferred_element_type=jnp.float32)
        - jnp.einsum("cfkb,cfk->fcb", fac_im, kept_im, preferred_element_type=jnp.float32)
    ) * factor_scale
    syn_im = (
        jnp.einsum("cfkb,cfk->fcb", fac_re, kept_im, preferred_element_type=jnp.float32)
        + jnp.einsum("cfkb,cfk->fcb", fac_im, kept_re, preferred_element_type=jnp.float32)
    ) * factor_scale
    synthesis = jnp.stack([syn_re, syn_im], axis=2).astype(jnp.bfloat16)
    returned = lax.all_to_all(synthesis, "freq", split_axis=0, concat_axis=1, tiled=True)
    filtered = jnp.einsum("sm,fspb->fpbm", placing_bf, returned, preferred_element_type=jnp.float32)
    return filtered.astype(jnp.bfloat16)


def solution(mesh):
    placed = (P("freq", None, "bl", None), P(), P(), P("freq", None, None, None, "bl"))
    return jax.shard_map(
        local, mesh=mesh, in_specs=placed, out_specs=P("freq", None, "bl", None), check_vma=False
    )
```

profile of v0, /device:TPU:0, one launch (start us, length us, event | category | flops | bytes accessed | tf_op | source)
XLA Modules:
  0.0 39.9 jit_solution(7122404698312272574)
XLA Ops:
  0.0 0.8 %multiply_convert_fusion = (bf16[2048,24]{0,1:T(8,128)(2,1)S(1)}, bf16[2048,24]{0,1:T(8,128)(2,1)S(1)}) fusion(), kind=kLoop, calls=%fused_computation.14 | loop fusion | flops 884736 | bytes 196608 | tf_op jit(solution)/shard_map/convert.9
  0.8 0.8 %copy-done = bf16[1,2,256,2048]{3,2,1,0:T(8,128)(2,1)S(1)} copy-done((bf16[1,2,256,2048]{3,2,1,0:T(8,128)(2,1)S(1)}, bf16[1,2,256,2048]{3,2,1,0:T(8,128)(2,1)}, u32[]{:S(2)}) %copy-start) | copy-done | bytes 2097176
  1.6 0.7 %convolution_bitcast_fusion = f32[512,48]{0,1:T(8,128)S(1)} fusion(bf16[512,2048]{1,0:T(8,128)(2,1)S(1)} %bitcast.100, bf16[2048,24]{0,1:T(8,128)(2,1)S(1)} %get-tuple-element.15, bf16[2048,24]{0,1:T(8,128)(2,1)S(1)} %get-tuple-element.16), kind=kOutput, calls=%fused_computation | convolution fusion | flops 101056512 | bytes 2392064 | tf_op jit(solution)/shard_map/dot_general | solution.py:24
  2.6 0.2 select_reduce_fusion
  2.9 0.3 fusion
  3.1 0.6 %copy.27 = bf16[1,32,2,256]{3,2,0,1:T(2,128)(2,1)} copy(bf16[1,32,2,256]{3,1,2,0:T(8,128)(2,1)S(1)} %fusion) | data formatting | bytes 65536 | tf_op jit(solution)/shard_map/convert_element_type | solution.py:58
  3.8 7.3 %all-to-all-start = ((bf16[1,32,2,256]{3,2,0,1:T(2,128)(2,1)}), bf16[1,32,2,256]{3,2,0,1:T(2,128)(2,1)S(1)}, u32[]{:S(2)}, u32[]{:S(2)}) async-start(bf16[1,32,2,256]{3,2,0,1:T(2,128)(2,1)} %copy.27), calls=%async_computation | async-start | bytes 65536 | tf_op jit(solution)/shard_map/all_to_all | solution.py:59
  11.2 0.3 fusion.43
  11.4 6.3 %all-to-all-done = bf16[1,32,2,256]{3,2,0,1:T(2,128)(2,1)S(1)} async-done(((bf16[1,32,2,256]{3,2,0,1:T(2,128)(2,1)}), bf16[1,32,2,256]{3,2,0,1:T(2,128)(2,1)S(1)}, u32[]{:S(2)}, u32[]{:S(2)}) %all-to-all-start) | async-done | bytes 32800 | tf_op jit(solution)/shard_map/all_to_all | solution.py:59
  17.8 0.1 fusion.29
  17.9 0.2 fusion.23
  18.1 0.2 fusion.25
  18.3 0.2 fusion.27
  18.4 0.1 copy.33
  18.5 0.1 copy.35
  18.8 10.1 %psum.7 = bf16[4,8,2,4]{1,3,0,2:T(4,128)(2,1)S(1)} all-reduce(f32[4,8,2,4]{1,3,0,2:T(4,128)S(1)} %pad_maximum_fusion.1), channel_id=1, replica_groups=mesh['freq'=8,'bl'=4] {'bl'}, use_global_device_ids=true, to_apply=%region_2.3 | all-reduce | flops 256 | bytes 1536 | tf_op jit(solution)/shard_map/psum | solution.py:73
  29.0 0.1 copy.41
  29.1 0.2 fusion.13
  29.3 0.2 fusion.15
  29.4 0.1 copy.38
  29.6 0.2 fusion.17
  29.7 0.2 fusion.11
  30.0 9.1 %all_to_all.21 = bf16[8,4,2,256]{3,1,2,0:T(4,128)(2,1)S(1)} all-to-all(bf16[8,4,2,256]{3,1,2,0:T(4,128)(2,1)S(1)} %pad_maximum_fusion), channel_id=1, replica_groups=mesh['freq'=8,'bl'=4] {'freq'}, dimensions={0} | all-to-all | bytes 65536 | tf_op jit(solution)/shard_map/all_to_all | solution.py:87
  39.1 0.8 %fusion.1 = bf16[1,2,256,24]{2,3,1,0:T(8,128)(2,1)} fusion(bf16[32,2,256]{2,0,1:T(8,128)(2,1)S(1)} %reshape.100, s32[24]{0:T(128)S(1)} %multiply_add_fusion), kind=kOutput, calls=%fused_computation.4 | convolution fusion | flops 799488 | bytes 57440 | tf_op jit(solution)/shard_map/sm,fspb->fpbm/dot_general | solution.py:88
  (32 shorter events, 0.8 us)
Async XLA Ops:
  0.0 1.6 %copy-start = (bf16[1,2,256,2048]{3,2,1,0:T(8,128)(2,1)S(1)}, bf16[1,2,256,2048]{3,2,1,0:T(8,128)(2,1)}, u32[]{:S(2)}) copy-start(bf16[1,2,256,2048]{3,2,1,0:T(8,128)(2,1)} %param.4) | copy-start | bytes 6291460
  0.0 2.5 %copy-start.3 = (s32[24,1]{0,1:T(1,128)S(1)}, s32[24,1]{0,1:T(1,128)}, u32[]{:S(2)}) copy-start(s32[24,1]{0,1:T(1,128)} %param.5) | copy-start | bytes 292
  0.0 11.1 %copy-start.1 = (bf16[4,8,2,4,256]{4,3,2,1,0:T(4,128)(2,1)S(1)}, bf16[4,8,2,4,256]{4,3,2,1,0:T(4,128)(2,1)}, u32[]{:S(2)}) copy-start(bf16[4,8,2,4,256]{4,3,2,1,0:T(4,128)(2,1)} %param.7) | copy-start | bytes 393220
  0.0 11.1 %copy-start.2 = (s32[24,8]{0,1:T(8,128)S(1)}, s32[24,8]{0,1:T(8,128)}, u32[]{:S(2)}) copy-start(s32[24,8]{0,1:T(8,128)} %param.6) | copy-start | bytes 2308
  3.8 13.9 %all-to-all-start = ((bf16[1,32,2,256]{3,2,0,1:T(2,128)(2,1)}), bf16[1,32,2,256]{3,2,0,1:T(2,128)(2,1)S(1)}, u32[]{:S(2)}, u32[]{:S(2)}) async-start(bf16[1,32,2,256]{3,2,0,1:T(2,128)(2,1)} %copy.27), calls=%async_computation | async-start | bytes 65536 | tf_op jit(solution)/shard_map/all_to_all | solution.py:59
where the time goes:
time: 40.1 us; the launch traced here: 39.9 us
  blocking collectives  19.2 us (48%)
  starting transfers between devices  7.25 us (18%)
  waiting for transfers between devices  6.27 us (16%)
  matrix products  3.32 us (8%)
  local copies, waits for them, and re-layouts  2.36 us (6%)
  other arithmetic  1.3 us (3%)
    psum x1, blocking collectives, local(): summed = lax.psum(partial_coef, 'bl')  10.1 us
    all_to_all x1, blocking collectives, local(): lax.all_to_all(synthesis, 'freq', split_axis=0, concat_axis=1, tiled=True)  9.06 us
    all_to_all x1, starting transfers between devices, local(): lax.all_to_all(outgoing, 'freq', split_axis=1, concat_axis=0, tiled=True)  7.25 us
    all_to_all x1, waiting for transfers between devices, local(): lax.all_to_all(outgoing, 'freq', split_axis=1, concat_axis=0, tiled=True)  6.27 us
  transfers between devices with their start and end apart: 1, of which 1 were waited for; matrix products, arithmetic and copies ran while one was open for 1% of the time, Pallas kernels for 0%

commit v1 on v0

v1 whole, which is shorter than its diff:
```python
import functools
import math

import jax
import jax.numpy as jnp
import numpy as np
from jax import lax
from jax.experimental import pallas as pl
from jax.experimental.pallas import tpu as pltpu
from jax.sharding import PartitionSpec as P

NB = 1024
CHUNKS = 4
F32 = jnp.float32
BF16 = jnp.bfloat16
MESH = pl.DeviceIdType.MESH


def wave_table(modes, half, samples):
    times = np.arange(samples, dtype=np.int64)[:, None]
    phases = times * np.arange(modes, dtype=np.int64)[None, :] % samples
    angles = phases * (2.0 * math.pi / samples)
    table = np.zeros((samples, 2 * half), np.float32)
    table[:, :modes] = np.cos(angles) / math.sqrt(samples)
    table[:, half : half + modes] = np.sin(angles) / math.sqrt(samples)
    return table.astype(BF16)


def flip(index, bits):
    place = 1
    while place <= bits:
        if bits & place:
            index = index + place * (1 - 2 * ((index // place) % 2))
        place *= 2
    return index


def kernel(
    dims, vis_ref, table_ref, owner_ref, counts_ref, factors_ref, out_ref,
    vis, table, held, spread, part, vis_sem, table_sem, send_sem, recv_sem, part_send, part_recv,
):
    n_freq, n_bl, modes, half, capacity, ranks = dims
    lanes = 2 * half
    rows = capacity * 2 * ranks
    group = min(n_freq, 8)
    deep = group * rows
    step = vis.shape[2]
    base_here = CHUNKS * step
    me = lax.axis_index("freq")
    mine = lax.axis_index("bl")

    def each_peer(body):
        if n_freq == 8:
            for bits in (6, 4, 7, 5, 2, 3, 1):
                other = flip(me, bits)
                body(bits, other, other)
        else:
            def turn(d, carry):
                body(d, lax.rem(me + d, n_freq), lax.rem(me + n_freq - d, n_freq))
                return carry

            lax.fori_loop(1, n_freq, turn, 0)

    barrier = pltpu.get_barrier_semaphore()

    def greet(d, to, source):
        pl.semaphore_signal(barrier, inc=1, device_id={"freq": to}, device_id_type=MESH)

    each_peer(greet)
    for d in range(1, n_bl):
        pl.semaphore_signal(
            barrier, inc=1, device_id={"bl": lax.rem(mine + d, n_bl)}, device_id_type=MESH
        )
    table_copy = pltpu.make_async_copy(table_ref, table, table_sem)
    table_copy.start()

    def vis_copy(c):
        rows_here = pl.ds(c * step, step)
        return pltpu.make_async_copy(vis_ref.at[0, :, rows_here], vis.at[:, c], vis_sem.at[c])

    for c in range(CHUNKS):
        vis_copy(c).start()
    pl.semaphore_wait(barrier, n_freq - 1 + n_bl - 1)

    def factor_copy(d, to, at):
        return pltpu.make_async_remote_copy(
            src_ref=factors_ref.at[to], dst_ref=held.at[at],
            send_sem=send_sem.at[d], recv_sem=recv_sem.at[d],
            device_id={"freq": to}, device_id_type=MESH,
        )

    each_peer(lambda d, to, source: factor_copy(d, to, me).start())
    held[me] = factors_ref[me]

    lane = lax.broadcasted_iota(jnp.int32, (modes, lanes), 1)
    mode = lax.broadcasted_iota(jnp.int32, (modes, lanes), 0)
    spreading = jnp.where(lane % half == mode, 1.0, 0.0).astype(BF16)
    owner_row = jnp.broadcast_to(owner_ref[...] + 1, (8, modes)).astype(F32).astype(BF16)
    owner_lanes = jnp.dot(owner_row, spreading, preferred_element_type=F32)[:1] - 1.0
    counts_row = jnp.broadcast_to(counts_ref[pl.ds(me, 1), :], (8, modes)).astype(F32).astype(BF16)
    counts_lanes = jnp.dot(counts_row, spreading, preferred_element_type=F32)
    owner_ids = lax.broadcasted_iota(jnp.int32, (n_freq, lanes), 0).astype(F32)
    onehot = jnp.where(owner_lanes == owner_ids, 1.0, 0.0)
    first = lax.broadcasted_iota(jnp.int32, (lanes, lanes), 0)
    second = lax.broadcasted_iota(jnp.int32, (lanes, lanes), 1)
    earlier = (first < second) & (first // half == second // half)
    earlier = jnp.where(earlier, 1.0, 0.0).astype(BF16)
    before = jnp.dot(onehot.astype(BF16), earlier, preferred_element_type=F32)
    ranking = jnp.sum(before * onehot, axis=0, keepdims=True)
    slot = owner_lanes * capacity + ranking
    slot_col = jnp.broadcast_to(slot, (8, lanes)).T[:, :1]
    scale = math.sqrt(NB / ranks)
    for g in range(n_freq // group):
        col = lax.broadcasted_iota(jnp.int32, (lanes, deep), 1) // (2 * ranks)
        col = (col + g * group * capacity).astype(F32)
        spread[g] = jnp.where(slot_col == col, scale, 0.0).astype(spread.dtype)

    table_copy.wait()
    pieces = []
    low = lax.broadcasted_iota(jnp.int32, (step, lanes), 1) < half
    for c in range(CHUNKS):
        vis_copy(c).wait()
        real = jnp.dot(vis[0, c], table[...], preferred_element_type=F32)
        imag = jnp.dot(vis[1, c], table[...], preferred_element_type=F32)
        piece = jnp.where(low, real, -real) + pltpu.roll(imag, half, 1)
        pieces.append(piece.astype(BF16))
    spectrum = jnp.concatenate(pieces, axis=0)

    each_peer(lambda d, to, source: factor_copy(d, to, source).wait_recv())
    total = jnp.zeros((2 * ranks, lanes), F32)
    for g in range(n_freq // group):
        factor = held[g * group : (g + 1) * group].reshape(deep, base_here)
        dense = jnp.dot(factor, spectrum, preferred_element_type=F32)
        row = lax.broadcasted_iota(jnp.int32, (deep, lanes), 0) // (2 * ranks)
        row = (row + g * group * capacity).astype(F32)
        chosen = jnp.where(slot == row, dense, 0.0)
        total = total + chosen.reshape(group * capacity, 2 * ranks, lanes).sum(axis=0)
    rank_row = lax.broadcasted_iota(jnp.int32, (2 * ranks, lanes), 0)
    in_low = lax.broadcasted_iota(jnp.int32, (2 * ranks, lanes), 1) < half
    crossed = pltpu.roll(pltpu.roll(total, ranks, 0), half, 1)
    part[mine] = total + jnp.where(in_low == (rank_row < ranks), crossed, -crossed)

    def part_copy(d, at):
        return pltpu.make_async_remote_copy(
            src_ref=part.at[mine], dst_ref=part.at[at],
            send_sem=part_send.at[d], recv_sem=part_recv.at[d],
            device_id={"bl": lax.rem(mine + d, n_bl)}, device_id_type=MESH,
        )

    for d in range(1, n_bl):
        part_copy(d, mine).start()
    for d in range(1, n_bl):
        part_copy(d, lax.rem(mine + n_bl - d, n_bl)).wait_recv()
    summed = part[0]
    for b in range(1, n_bl):
        summed = summed + part[b]
    kept = jnp.where((rank_row % ranks).astype(F32) < counts_lanes, summed, 0.0).astype(BF16)

    tiling = lax.broadcasted_iota(jnp.int32, (2 * ranks, deep), 1) % (2 * ranks)
    tiling = jnp.where(
        tiling == lax.broadcasted_iota(jnp.int32, (2 * ranks, deep), 0), 1.0, 0.0
    ).astype(BF16)
    tiled = lax.dot_general(
        kept, tiling, (((0,), (0,)), ((), ())), preferred_element_type=F32
    )
    filtered = jnp.zeros((lanes, base_here), F32)
    for g in range(n_freq // group):
        factor = held[g * group : (g + 1) * group].reshape(deep, base_here)
        weight = (tiled * spread[g].astype(F32)).astype(BF16)
        filtered = filtered + jnp.dot(weight, factor, preferred_element_type=F32)
    filtered = filtered.astype(BF16)
    out_ref[0] = filtered[:modes]
    out_ref[1] = filtered[half : half + modes]
    each_peer(lambda d, to, source: factor_copy(d, to, me).wait_send())
    for d in range(1, n_bl):
        part_copy(d, mine).wait_send()


def local(n_freq, n_bl, vis_time, owner, counts, factors):
    _, _, base_here, samples = vis_time.shape
    modes = owner.shape[0]
    capacity, _, _, ranks, _ = factors.shape
    half = -(-2 * modes // 128) * 64
    rows = capacity * 2 * ranks
    group = min(n_freq, 8)
    table = jnp.asarray(wave_table(modes, half, samples))
    moved = factors.transpose(1, 0, 2, 3, 4).reshape(n_freq, rows, base_here)
    vmem = pl.BlockSpec(memory_space=pltpu.VMEM)
    anywhere = pl.BlockSpec(memory_space=pl.ANY)
    out = pl.pallas_call(
        functools.partial(kernel, (n_freq, n_bl, modes, half, capacity, ranks)),
        out_shape=jax.ShapeDtypeStruct((2, modes, base_here), BF16),
        in_specs=[anywhere, anywhere, vmem, vmem, vmem],
        out_specs=vmem,
        scratch_shapes=[
            pltpu.VMEM((2, CHUNKS, base_here // CHUNKS, samples), BF16),
            pltpu.VMEM((samples, 2 * half), BF16),
            pltpu.VMEM((n_freq, rows, base_here), BF16),
            pltpu.VMEM((n_freq // group, 2 * half, group * rows), BF16),
            pltpu.VMEM((n_bl, 2 * ranks, 2 * half), F32),
            pltpu.SemaphoreType.DMA((CHUNKS,)),
            pltpu.SemaphoreType.DMA,
            pltpu.SemaphoreType.DMA((n_freq,)),
            pltpu.SemaphoreType.DMA((n_freq,)),
            pltpu.SemaphoreType.DMA((n_bl,)),
            pltpu.SemaphoreType.DMA((n_bl,)),
        ],
        compiler_params=pltpu.CompilerParams(
            collective_id=0, has_side_effects=True, vmem_limit_bytes=48 * 1024 * 1024
        ),
    )(vis_time, table, owner.T, counts.T, moved)
    return out.transpose(0, 2, 1)[None]


def solution(mesh):
    placed = (P("freq", None, "bl", None), P(), P(), P("freq", None, None, None, "bl"))
    return jax.shard_map(
        functools.partial(local, mesh.shape["freq"], mesh.shape["bl"]),
        mesh=mesh, in_specs=placed, out_specs=P("freq", None, "bl", None), check_vma=False,
    )
```

time: 40.1 us -> 19.6 us (0.49)
  blocking collectives: 19.2 us -> 0 us
  Pallas kernels: 0 us -> 13.7 us
  starting transfers between devices: 7.25 us -> 0 us
  waiting for transfers between devices: 6.27 us -> 0 us
  matrix products: 3.32 us -> 0 us
  local copies, waits for them, and re-layouts: 2.36 us -> 5.57 us
  other arithmetic: 1.3 us -> 0 us
    pallas_call x0 -> x1, Pallas kernels: none -> 13.7 us  [local(): pl.pallas_call(functools.partial(kernel, (n_freq, n_bl, modes, half, capa...]
    psum x1 -> x0, blocking collectives: 10.1 us -> none  [local(): summed = lax.psum(partial_coef, 'bl')]
    all_to_all x1 -> x0, blocking collectives: 9.06 us -> none  [local(): lax.all_to_all(synthesis, 'freq', split_axis=0, concat_axis=1, tiled=True)]
    all_to_all x1 -> x0, starting transfers between devices: 7.25 us -> none  [local(): lax.all_to_all(outgoing, 'freq', split_axis=1, concat_axis=0, tiled=True)]
    all_to_all x1 -> x0, waiting for transfers between devices: 6.27 us -> none  [local(): lax.all_to_all(outgoing, 'freq', split_axis=1, concat_axis=0, tiled=True)]
    unnamed x8 -> x9, local copies, waits for them, and re-layouts: 0.79 us -> 4.58 us
    dot_general x12 -> x0, matrix products: 3.32 us -> none  [the longest x1 0.8 us: local(): jnp.einsum('sm,fspb->fpbm', placing_bf, returned, preferred_element_type=...]
    transpose x0 -> x1, local copies, waits for them, and re-layouts: none -> 0.95 us  [local(): moved = factors.transpose(1, 0, 2, 3, 4).reshape(n_freq, rows, base_here)]
  transfers between devices with their start and end apart: 1 -> 0, of which waited for: 1 -> 0; matrix products, arithmetic and copies ran while one was open for 1% -> 0% of each run, Pallas kernels for 0% -> 0%
where the time goes in v1:
time: 19.6 us; the launch traced here: 19.3 us
  Pallas kernels  13.7 us (70%)
  local copies, waits for them, and re-layouts  5.57 us (28%)
    pallas_call x1, Pallas kernels, local(): pl.pallas_call(functools.partial(kernel, (n_freq, n_bl, modes, half, capa...  13.7 us
    unnamed x9, local copies, waits for them, and re-layouts  4.58 us
    transpose x1, local copies, waits for them, and re-layouts, local(): moved = factors.transpose(1, 0, 2, 3, 4).reshape(n_freq, rows, base_here)  0.95 us

profile of v1, /device:TPU:0, one launch (start us, length us, event | category | flops | bytes accessed | tf_op | source)
XLA Modules:
  0.0 19.3 jit_solution(894294782210944557)
XLA Ops:
  0.0 0.9 %copy.6 = bf16[8,4,2,4,256]{4,3,2,1,0:T(4,128)(2,1)S(1)} copy(bf16[8,4,2,4,256]{4,3,2,0,1:T(4,128)(2,1)} %bitcast.9) | data formatting | bytes 262144 | tf_op jit(solution)/shard_map/transpose | solution.py:187
  1.0 0.0 copy-start
  1.0 1.6 %copy-done = bf16[1,2,256,2048]{3,2,1,0:T(8,128)(2,1)S(1)} copy-done((bf16[1,2,256,2048]{3,2,1,0:T(8,128)(2,1)S(1)}, bf16[1,2,256,2048]{3,2,1,0:T(8,128)(2,1)}, u32[]{:S(2)}) %copy-start) | copy-done | bytes 2097176
  2.6 0.0 copy-start.1
  2.6 1.0 %copy-done.1 = bf16[2048,128]{1,0:T(8,128)(2,1)S(1)} copy-done((bf16[2048,128]{1,0:T(8,128)(2,1)S(1)}, bf16[2048,128]{1,0:T(8,128)(2,1)}, u32[]{:S(2)}) %copy-start.1) | copy-done | bytes 524312
  3.6 0.0 copy-start.2
  3.6 0.7 %copy-done.2 = s32[24,8]{0,1:T(8,128)S(1)} copy-done((s32[24,8]{0,1:T(8,128)S(1)}, s32[24,8]{0,1:T(8,128)}, u32[]{:S(2)}) %copy-start.2) | copy-done | bytes 792
  4.3 0.0 copy-start.3
  4.3 0.7 %copy-done.3 = s32[24,1]{0,1:T(1,128)S(1)} copy-done((s32[24,1]{0,1:T(1,128)S(1)}, s32[24,1]{0,1:T(1,128)}, u32[]{:S(2)}) %copy-start.3) | copy-done | bytes 120
  5.0 13.7 %shard_map.55 = bf16[2,24,256]{2,1,0:T(8,128)(2,1)S(1)} custom-call(bf16[1,2,256,2048]{3,2,1,0:T(8,128)(2,1)S(1)} %copy-done, bf16[2048,128]{1,0:T(8,128)(2,1)S(1)} %copy-done.1, s32[1,24]{1,0:T(1,128)S(1)} %bitcast.8, s32[8,24]{1,0:T(8,128)S(1)} %bitcast.7, bf16[8,32,256]{2,1,0:T(8,128)(2,1)S(1)} %reshape.3.factors_ref), custom_call_target="tpu_custom_call" | custom-call | tf_op jit(solution)/shard_map/pallas_call | solution.py:190
  18.7 0.6 %copy.8 = bf16[1,2,256,24]{2,3,1,0:T(8,128)(2,1)} copy(bf16[1,2,256,24]{2,3,1,0:T(8,128)(2,1)S(1)} %bitcast.6) | data formatting | bytes 49152
  (1 shorter events, 0.0 us)
Async XLA Ops:
  1.0 1.6 %copy-start = (bf16[1,2,256,2048]{3,2,1,0:T(8,128)(2,1)S(1)}, bf16[1,2,256,2048]{3,2,1,0:T(8,128)(2,1)}, u32[]{:S(2)}) copy-start(bf16[1,2,256,2048]{3,2,1,0:T(8,128)(2,1)} %vis_ref.1) | copy-start | bytes 6291460
  2.6 1.0 %copy-start.1 = (bf16[2048,128]{1,0:T(8,128)(2,1)S(1)}, bf16[2048,128]{1,0:T(8,128)(2,1)}, u32[]{:S(2)}) copy-start(bf16[2048,128]{1,0:T(8,128)(2,1)} %constant.2.clone.table_ref) | copy-start | bytes 1572868
  3.6 0.7 %copy-start.2 = (s32[24,8]{0,1:T(8,128)S(1)}, s32[24,8]{0,1:T(8,128)}, u32[]{:S(2)}) copy-start(s32[24,8]{0,1:T(8,128)} %param.7) | copy-start | bytes 2308
  4.3 0.7 %copy-start.3 = (s32[24,1]{0,1:T(1,128)S(1)}, s32[24,1]{0,1:T(1,128)}, u32[]{:S(2)}) copy-start(s32[24,1]{0,1:T(1,128)} %param.6) | copy-start | bytes 292

commit v2 on v1

v2 whole, which is shorter than its diff:
```python
import functools
import math

import jax
import jax.numpy as jnp
import numpy as np
from jax import lax
from jax.experimental import pallas as pl
from jax.experimental.pallas import tpu as pltpu
from jax.sharding import PartitionSpec as P

NB = 1024
CHUNKS = 4
F32 = jnp.float32
BF16 = jnp.bfloat16
MESH = pl.DeviceIdType.MESH


def wave_table(modes, half, samples):
    times = np.arange(samples, dtype=np.int64)[:, None]
    phases = times * np.arange(modes, dtype=np.int64)[None, :] % samples
    angles = phases * (2.0 * math.pi / samples)
    table = np.zeros((samples, 2 * half), np.float32)
    table[:, :modes] = np.cos(angles) / math.sqrt(samples)
    table[:, half : half + modes] = np.sin(angles) / math.sqrt(samples)
    return table.astype(BF16)


def flip(index, bits):
    place = 1
    while place <= bits:
        if bits & place:
            index = index + place * (1 - 2 * ((index // place) % 2))
        place *= 2
    return index


def kernel(
    dims, vis_ref, table_ref, owner_ref, counts_ref, factors_ref, out_ref,
    vis, table, owner, counts, held, packed, spread, part,
    vis_sem, table_sem, small_sem, send_sem, recv_sem, part_send, part_recv,
):
    n_freq, n_bl, modes, half, capacity, ranks = dims
    lanes = 2 * half
    rows = capacity * 2 * ranks
    group = min(n_freq // 2, 4)
    deep = group * rows
    blocks = n_freq // group
    base_here, step = vis.shape[2], vis.shape[3]
    me = lax.axis_index("freq")
    mine = lax.axis_index("bl")

    def peers(body, chosen=None):
        if n_freq == 8:
            for bits in chosen or (6, 4, 7, 5, 2, 3, 1):
                other = flip(me, bits)
                body(bits, other, other)
        elif chosen is None or chosen[0] == 1:
            def turn(d, carry):
                body(d, lax.rem(me + d, n_freq), lax.rem(me + n_freq - d, n_freq))
                return carry

            lax.fori_loop(1, n_freq, turn, 0)

    barrier = pltpu.get_barrier_semaphore()

    def greet(d, to, source):
        pl.semaphore_signal(barrier, inc=1, device_id={"freq": to}, device_id_type=MESH)

    peers(greet)
    for d in range(1, n_bl):
        pl.semaphore_signal(
            barrier, inc=1, device_id={"bl": lax.rem(mine + d, n_bl)}, device_id_type=MESH
        )

    def vis_copy(c):
        return pltpu.make_async_copy(
            vis_ref.at[0, :, :, pl.ds(c * step, step)], vis.at[c], vis_sem.at[c]
        )

    def table_copy(c):
        times = pl.ds(c * step, step)
        return pltpu.make_async_copy(table_ref.at[times], table.at[times], table_sem.at[c])

    owner_copy = pltpu.make_async_copy(owner_ref, owner, small_sem.at[0])
    counts_copy = pltpu.make_async_copy(counts_ref, counts, small_sem.at[1])
    own_copy = pltpu.make_async_copy(factors_ref.at[:, me], held.at[me], small_sem.at[2])
    owner_copy.start()
    counts_copy.start()
    for c in range(CHUNKS):
        table_copy(c).start()
        vis_copy(c).start()
    own_copy.start()
    pl.semaphore_wait(barrier, n_freq - 1 + n_bl - 1)

    def factor_copy(d, to, at):
        return pltpu.make_async_remote_copy(
            src_ref=factors_ref.at[:, to], dst_ref=held.at[at],
            send_sem=send_sem.at[d], recv_sem=recv_sem.at[d],
            device_id={"freq": to}, device_id_type=MESH,
        )

    peers(lambda d, to, source: factor_copy(d, to, me).start())

    owner_copy.wait()
    counts_copy.wait()
    lane = lax.broadcasted_iota(jnp.int32, (modes, lanes), 1)
    mode = lax.broadcasted_iota(jnp.int32, (modes, lanes), 0)
    spreading = jnp.where(lane % half == mode, 1.0, 0.0).astype(BF16)
    owner_row = jnp.broadcast_to(owner[...] + 1, (8, modes)).astype(F32).astype(BF16)
    owner_lanes = jnp.dot(owner_row, spreading, preferred_element_type=F32)[:1] - 1.0
    counts_row = jnp.broadcast_to(counts[pl.ds(me, 1), :], (8, modes)).astype(F32).astype(BF16)
    counts_lanes = jnp.dot(counts_row, spreading, preferred_element_type=F32)
    owner_ids = lax.broadcasted_iota(jnp.int32, (n_freq, lanes), 0).astype(F32)
    onehot = jnp.where(owner_lanes == owner_ids, 1.0, 0.0)
    first = lax.broadcasted_iota(jnp.int32, (lanes, lanes), 0)
    second = lax.broadcasted_iota(jnp.int32, (lanes, lanes), 1)
    earlier = (first < second) & (first // half == second // half)
    earlier = jnp.where(earlier, 1.0, 0.0).astype(BF16)
    before = jnp.dot(onehot.astype(BF16), earlier, preferred_element_type=F32)
    ranking = jnp.sum(before * onehot, axis=0, keepdims=True)
    slot = owner_lanes * capacity + ranking
    slot_col = jnp.broadcast_to(slot, (8, lanes)).T[:, :1]
    scale = math.sqrt(NB / ranks)
    for g in range(blocks):
        col = lax.broadcasted_iota(jnp.int32, (lanes, deep), 1) // (2 * ranks)
        col = (col + g * group * capacity).astype(F32)
        spread[g] = jnp.where(slot_col == col, scale, 0.0).astype(spread.dtype)

    spectra = jnp.zeros((2 * base_here, lanes), F32)
    for c in range(CHUNKS):
        table_copy(c).wait()
        vis_copy(c).wait()
        spectra = spectra + jnp.dot(
            vis[c].reshape(2 * base_here, step), table[c * step : (c + 1) * step],
            preferred_element_type=F32,
        )
    real, imag = spectra[:base_here], spectra[base_here:]
    low = lax.broadcasted_iota(jnp.int32, (base_here, lanes), 1) < half
    spectrum = (jnp.where(low, real, -real) + pltpu.roll(imag, half, 1)).astype(BF16)

    def coefficients(block):
        from_here = pl.ds(block * group, group)
        factor = held[from_here].reshape(deep, base_here)
        packed[block] = factor
        dense = jnp.dot(factor, spectrum, preferred_element_type=F32)
        row = lax.broadcasted_iota(jnp.int32, (deep, lanes), 0) // (2 * ranks)
        row = (row + block * group * capacity).astype(F32)
        chosen = jnp.where(slot == row, dense, 0.0)
        return chosen.reshape(group * capacity, 2 * ranks, lanes).sum(axis=0)

    own_copy.wait()
    total = jnp.zeros((2 * ranks, lanes), F32)
    peers(lambda d, to, source: factor_copy(d, to, source).wait_recv(), (1, 2, 3))
    for b in range(blocks):
        if b == 1:
            peers(lambda d, to, source: factor_copy(d, to, source).wait_recv(), (4, 5, 6, 7))
        total = total + coefficients(lax.rem(me // group + b, blocks))
    rank_row = lax.broadcasted_iota(jnp.int32, (2 * ranks, lanes), 0)
    in_low = lax.broadcasted_iota(jnp.int32, (2 * ranks, lanes), 1) < half
    crossed = pltpu.roll(pltpu.roll(total, ranks, 0), half, 1)
    part[mine] = total + jnp.where(in_low == (rank_row < ranks), crossed, -crossed)

    def part_copy(d, at):
        return pltpu.make_async_remote_copy(
            src_ref=part.at[mine], dst_ref=part.at[at],
            send_sem=part_send.at[d], recv_sem=part_recv.at[d],
            device_id={"bl": lax.rem(mine + d, n_bl)}, device_id_type=MESH,
        )

    for d in range(1, n_bl):
        part_copy(d, mine).start()
    for d in range(1, n_bl):
        part_copy(d, lax.rem(mine + n_bl - d, n_bl)).wait_recv()
    summed = part[0]
    for b in range(1, n_bl):
        summed = summed + part[b]
    kept = jnp.where((rank_row % ranks).astype(F32) < counts_lanes, summed, 0.0).astype(BF16)

    tiling = lax.broadcasted_iota(jnp.int32, (2 * ranks, deep), 1) % (2 * ranks)
    tiling = jnp.where(
        tiling == lax.broadcasted_iota(jnp.int32, (2 * ranks, deep), 0), 1.0, 0.0
    ).astype(BF16)
    tiled = lax.dot_general(
        kept, tiling, (((0,), (0,)), ((), ())), preferred_element_type=F32
    )
    filtered = jnp.zeros((lanes, base_here), F32)
    for g in range(blocks):
        weight = (tiled * spread[g].astype(F32)).astype(BF16)
        filtered = filtered + jnp.dot(weight, packed[g], preferred_element_type=F32)
    filtered = filtered.astype(BF16)
    out_ref[0] = filtered[:modes]
    out_ref[1] = filtered[half : half + modes]
    peers(lambda d, to, source: factor_copy(d, to, me).wait_send())
    for d in range(1, n_bl):
        part_copy(d, mine).wait_send()


def local(n_freq, n_bl, vis_time, owner, counts, factors):
    _, _, base_here, samples = vis_time.shape
    modes = owner.shape[0]
    capacity, _, _, ranks, _ = factors.shape
    half = -(-2 * modes // 128) * 64
    rows = capacity * 2 * ranks
    group = min(n_freq // 2, 4)
    table = jnp.asarray(wave_table(modes, half, samples))
    stays = pl.BlockSpec(memory_space=pltpu.HBM)
    out = pl.pallas_call(
        functools.partial(kernel, (n_freq, n_bl, modes, half, capacity, ranks)),
        out_shape=jax.ShapeDtypeStruct((2, modes, base_here), BF16),
        in_specs=[stays] * 5,
        out_specs=pl.BlockSpec(memory_space=pltpu.VMEM),
        scratch_shapes=[
            pltpu.VMEM((CHUNKS, 2, base_here, samples // CHUNKS), BF16),
            pltpu.VMEM((samples, 2 * half), BF16),
            pltpu.VMEM((1, modes), jnp.int32),
            pltpu.VMEM((n_freq, modes), jnp.int32),
            pltpu.VMEM((n_freq, capacity, 2, ranks, base_here), BF16),
            pltpu.VMEM((n_freq // group, group * rows, base_here), BF16),
            pltpu.VMEM((n_freq // group, 2 * half, group * rows), BF16),
            pltpu.VMEM((n_bl, 2 * ranks, 2 * half), F32),
            pltpu.SemaphoreType.DMA((CHUNKS,)),
            pltpu.SemaphoreType.DMA((CHUNKS,)),
            pltpu.SemaphoreType.DMA((3,)),
            pltpu.SemaphoreType.DMA((n_freq,)),
            pltpu.SemaphoreType.DMA((n_freq,)),
            pltpu.SemaphoreType.DMA((n_bl,)),
            pltpu.SemaphoreType.DMA((n_bl,)),
        ],
        compiler_params=pltpu.CompilerParams(
            collective_id=0, has_side_effects=True, vmem_limit_bytes=63 * 1024 * 1024
        ),
    )(vis_time, table, owner.T, counts.T, factors)
    return out.transpose(0, 2, 1)[None]


def solution(mesh):
    placed = (P("freq", None, "bl", None), P(), P(), P("freq", None, None, None, "bl"))
    return jax.shard_map(
        functools.partial(local, mesh.shape["freq"], mesh.shape["bl"]),
        mesh=mesh, in_specs=placed, out_specs=P("freq", None, "bl", None), check_vma=False,
    )
```

time: 19.6 us -> 16.1 us (0.82)
  local copies, waits for them, and re-layouts: 5.57 us -> 1.35 us
  Pallas kernels: 13.7 us -> 14.6 us
    unnamed x9 -> x1, local copies, waits for them, and re-layouts: 4.58 us -> 1.35 us
    transpose x1 -> x0, local copies, waits for them, and re-layouts: 0.95 us -> none  [local(): moved = factors.transpose(1, 0, 2, 3, 4).reshape(n_freq, rows, base_here)]
    pallas_call x1, Pallas kernels: 13.7 us -> 14.6 us  [local(): pl.pallas_call(functools.partial(kernel, (n_freq, n_bl, modes, half, capa...]
where the time goes in v2:
time: 16.1 us; the launch traced here: 15.9 us
  Pallas kernels  14.6 us (91%)
  local copies, waits for them, and re-layouts  1.35 us (8%)
    pallas_call x1, Pallas kernels, local(): pl.pallas_call(functools.partial(kernel, (n_freq, n_bl, modes, half, capa...  14.6 us
    unnamed x1, local copies, waits for them, and re-layouts  1.35 us

profile of v2, /device:TPU:0, one launch (start us, length us, event | category | flops | bytes accessed | tf_op | source)
XLA Modules:
  0.0 15.9 jit_solution(8550820970113481781)
XLA Ops:
  0.0 14.6 %shard_map.55 = bf16[2,24,256]{2,1,0:T(8,128)(2,1)} custom-call(bf16[1,2,256,2048]{3,2,1,0:T(8,128)(2,1)} %vis_ref.1, bf16[2048,128]{1,0:T(8,128)(2,1)} %constant.2.clone.table_ref, s32[1,24]{1,0:T(1,128)} %bitcast.7, s32[8,24]{1,0:T(8,128)} %bitcast.6, bf16[4,8,2,4,256]{4,3,2,1,0:T(4,128)(2,1)} %factors_ref.1), custom_call_target="tpu_custom_call" | custom-call | tf_op jit(solution)/shard_map/pallas_call | solution.py:208
  14.6 1.3 %copy.7 = bf16[1,2,256,24]{2,3,1,0:T(8,128)(2,1)} copy(bf16[1,2,256,24]{2,3,1,0:T(8,128)(2,1)} %bitcast.5) | data formatting | bytes 49152

commit v3 on v2

--- a/solution.py
+++ b/solution.py
@@ -207,7 +207,7 @@
     stays = pl.BlockSpec(memory_space=pltpu.HBM)
     out = pl.pallas_call(
         functools.partial(kernel, (n_freq, n_bl, modes, half, capacity, ranks)),
-        out_shape=jax.ShapeDtypeStruct((2, modes, base_here), BF16),
+        out_shape=pltpu.VMEM((2, modes, base_here), BF16),
         in_specs=[stays] * 5,
         out_specs=pl.BlockSpec(memory_space=pltpu.VMEM),
         scratch_shapes=[

time: 16.1 us -> 14.8 us (0.919)
  local copies, waits for them, and re-layouts: 1.35 us -> 0.61 us
  Pallas kernels: 14.6 us -> 14 us
    unnamed x1, local copies, waits for them, and re-layouts: 1.35 us -> 0.61 us
    pallas_call x1, Pallas kernels: 14.6 us -> 14 us  [local(): pl.pallas_call(functools.partial(kernel, (n_freq, n_bl, modes, half, capa...]
where the time goes in v3:
time: 14.8 us; the launch traced here: 14.6 us
  Pallas kernels  14 us (95%)
  local copies, waits for them, and re-layouts  0.61 us (4%)
    pallas_call x1, Pallas kernels, local(): pl.pallas_call(functools.partial(kernel, (n_freq, n_bl, modes, half, capa...  14 us
    unnamed x1, local copies, waits for them, and re-layouts  0.61 us

profile of v3, /device:TPU:0, one launch (start us, length us, event | category | flops | bytes accessed | tf_op | source)
XLA Modules:
  0.0 14.6 jit_solution(13720922995919627869)
XLA Ops:
  0.0 14.0 %shard_map.55 = bf16[2,24,256]{2,1,0:T(8,128)(2,1)S(1)} custom-call(bf16[1,2,256,2048]{3,2,1,0:T(8,128)(2,1)} %vis_ref.1, bf16[2048,128]{1,0:T(8,128)(2,1)} %constant.2.clone.table_ref, s32[1,24]{1,0:T(1,128)} %bitcast.7, s32[8,24]{1,0:T(8,128)} %bitcast.6, bf16[4,8,2,4,256]{4,3,2,1,0:T(4,128)(2,1)} %factors_ref.1), custom_call_target="tpu_custom_call" | custom-call | tf_op jit(solution)/shard_map/pallas_call | solution.py:208
  14.0 0.6 %copy.7 = bf16[1,2,256,24]{2,3,1,0:T(8,128)(2,1)} copy(bf16[1,2,256,24]{2,3,1,0:T(8,128)(2,1)S(1)} %bitcast.5) | data formatting | bytes 49152

commit v4 on v3

--- a/solution.py
+++ b/solution.py
@@ -10,7 +10,7 @@
 from jax.sharding import PartitionSpec as P
 
 NB = 1024
-CHUNKS = 4
+CHUNKS = 2
 F32 = jnp.float32
 BF16 = jnp.bfloat16
 MESH = pl.DeviceIdType.MESH
@@ -37,7 +37,7 @@
 
 def kernel(
     dims, vis_ref, table_ref, owner_ref, counts_ref, factors_ref, out_ref,
-    vis, table, owner, counts, held, packed, spread, part,
+    vis, table, owner, counts, held, packed, spread, slots, limits, spectrum, part,
     vis_sem, table_sem, small_sem, send_sem, recv_sem, part_send, part_recv,
 ):
     n_freq, n_bl, modes, half, capacity, ranks = dims
@@ -85,13 +85,14 @@
     owner_copy = pltpu.make_async_copy(owner_ref, owner, small_sem.at[0])
     counts_copy = pltpu.make_async_copy(counts_ref, counts, small_sem.at[1])
     own_copy = pltpu.make_async_copy(factors_ref.at[:, me], held.at[me], small_sem.at[2])
-    owner_copy.start()
-    counts_copy.start()
-    for c in range(CHUNKS):
-        table_copy(c).start()
-        vis_copy(c).start()
-    own_copy.start()
-    pl.semaphore_wait(barrier, n_freq - 1 + n_bl - 1)
+
+    def fetch():
+        for c in range(CHUNKS):
+            table_copy(c).start()
+            vis_copy(c).start()
+        owner_copy.start()
+        counts_copy.start()
+        own_copy.start()
 
     def factor_copy(d, to, at):
         return pltpu.make_async_remote_copy(
@@ -100,50 +101,66 @@
             device_id={"freq": to}, device_id_type=MESH,
         )
 
+    def prepare():
+        owner_copy.wait()
+        counts_copy.wait()
+        lane = lax.broadcasted_iota(jnp.int32, (modes, lanes), 1)
+        mode = lax.broadcasted_iota(jnp.int32, (modes, lanes), 0)
+        spreading = jnp.where(lane % half == mode, 1.0, 0.0).astype(BF16)
+        owner_row = jnp.broadcast_to(owner[...] + 1, (8, modes)).astype(F32).astype(BF16)
+        owner_lanes = jnp.dot(owner_row, spreading, preferred_element_type=F32)[:1] - 1.0
+        counts_row = jnp.broadcast_to(counts[pl.ds(me, 1), :], (8, modes)).astype(F32).astype(BF16)
+        limits[...] = jnp.dot(counts_row, spreading, preferred_element_type=F32)
+        owner_ids = lax.broadcasted_iota(jnp.int32, (n_freq, lanes), 0).astype(F32)
+        onehot = jnp.where(owner_lanes == owner_ids, 1.0, 0.0)
+        first = lax.broadcasted_iota(jnp.int32, (lanes, lanes), 0)
+        second = lax.broadcasted_iota(jnp.int32, (lanes, lanes), 1)
+        earlier = (first < second) & (first // half == second // half)
+        earlier = jnp.where(earlier, 1.0, 0.0).astype(BF16)
+        before = jnp.dot(onehot.astype(BF16), earlier, preferred_element_type=F32)
+        ranking = jnp.sum(before * onehot, axis=0, keepdims=True)
+        slot = owner_lanes * capacity + ranking
+        slots[...] = jnp.broadcast_to(slot, (8, lanes))
+        slot_col = jnp.broadcast_to(slot, (8, lanes)).T[:, :1]
+        scale = math.sqrt(NB / ranks)
+        for g in range(blocks):
+            col = lax.broadcasted_iota(jnp.int32, (lanes, deep), 1) // (2 * ranks)
+            col = (col + g * group * capacity).astype(F32)
+            spread[g] = jnp.where(slot_col == col, scale, 0.0).astype(spread.dtype)
+
+        spectra = jnp.zeros((2 * base_here, lanes), F32)
+        for c in range(CHUNKS):
+            table_copy(c).wait()
+            vis_copy(c).wait()
+            spectra = spectra + jnp.dot(
+                vis[c].reshape(2 * base_here, step), table[c * step : (c + 1) * step],
+                preferred_element_type=F32,
+            )
+        real, imag = spectra[:base_here], spectra[base_here:]
+        low = lax.broadcasted_iota(jnp.int32, (base_here, lanes), 1) < half
+        spectrum[...] = (jnp.where(low, real, -real) + pltpu.roll(imag, half, 1)).astype(BF16)
+
+    leading = me < n_freq // 2
+
+    @pl.when(leading)
+    def _():
+        fetch()
+        prepare()
+
+    pl.semaphore_wait(barrier, n_freq - 1 + n_bl - 1)
     peers(lambda d, to, source: factor_copy(d, to, me).start())
 
-    owner_copy.wait()
-    counts_copy.wait()
-    lane = lax.broadcasted_iota(jnp.int32, (modes, lanes), 1)
-    mode = lax.broadcasted_iota(jnp.int32, (modes, lanes), 0)
-    spreading = jnp.where(lane % half == mode, 1.0, 0.0).astype(BF16)
-    owner_row = jnp.broadcast_to(owner[...] + 1, (8, modes)).astype(F32).astype(BF16)
-    owner_lanes = jnp.dot(owner_row, spreading, preferred_element_type=F32)[:1] - 1.0
-    counts_row = jnp.broadcast_to(counts[pl.ds(me, 1), :], (8, modes)).astype(F32).astype(BF16)
-    counts_lanes = jnp.dot(counts_row, spreading, preferred_element_type=F32)
-    owner_ids = lax.broadcasted_iota(jnp.int32, (n_freq, lanes), 0).astype(F32)
-    onehot = jnp.where(owner_lanes == owner_ids, 1.0, 0.0)
-    first = lax.broadcasted_iota(jnp.int32, (lanes, lanes), 0)
-    second = lax.broadcasted_iota(jnp.int32, (lanes, lanes), 1)
-    earlier = (first < second) & (first // half == second // half)
-    earlier = jnp.where(earlier, 1.0, 0.0).astype(BF16)
-    before = jnp.dot(onehot.astype(BF16), earlier, preferred_element_type=F32)
-    ranking = jnp.sum(before * onehot, axis=0, keepdims=True)
-    slot = owner_lanes * capacity + ranking
-    slot_col = jnp.broadcast_to(slot, (8, lanes)).T[:, :1]
-    scale = math.sqrt(NB / ranks)
-    for g in range(blocks):
-        col = lax.broadcasted_iota(jnp.int32, (lanes, deep), 1) // (2 * ranks)
-        col = (col + g * group * capacity).astype(F32)
-        spread[g] = jnp.where(slot_col == col, scale, 0.0).astype(spread.dtype)
-
-    spectra = jnp.zeros((2 * base_here, lanes), F32)
-    for c in range(CHUNKS):
-        table_copy(c).wait()
-        vis_copy(c).wait()
-        spectra = spectra + jnp.dot(
-            vis[c].reshape(2 * base_here, step), table[c * step : (c + 1) * step],
-            preferred_element_type=F32,
-        )
-    real, imag = spectra[:base_here], spectra[base_here:]
-    low = lax.broadcasted_iota(jnp.int32, (base_here, lanes), 1) < half
-    spectrum = (jnp.where(low, real, -real) + pltpu.roll(imag, half, 1)).astype(BF16)
-
+    @pl.when(jnp.logical_not(leading))
+    def _():
+        fetch()
+        prepare()
+
+    slot = slots[:1]
     def coefficients(block):
         from_here = pl.ds(block * group, group)
         factor = held[from_here].reshape(deep, base_here)
         packed[block] = factor
-        dense = jnp.dot(factor, spectrum, preferred_element_type=F32)
+        dense = jnp.dot(factor, spectrum[...], preferred_element_type=F32)
         row = lax.broadcasted_iota(jnp.int32, (deep, lanes), 0) // (2 * ranks)
         row = (row + block * group * capacity).astype(F32)
         chosen = jnp.where(slot == row, dense, 0.0)
@@ -175,7 +192,7 @@
     summed = part[0]
     for b in range(1, n_bl):
         summed = summed + part[b]
-    kept = jnp.where((rank_row % ranks).astype(F32) < counts_lanes, summed, 0.0).astype(BF16)
+    kept = jnp.where((rank_row % ranks).astype(F32) < limits[:2 * ranks], summed, 0.0).astype(BF16)
 
     tiling = lax.broadcasted_iota(jnp.int32, (2 * ranks, deep), 1) % (2 * ranks)
     tiling = jnp.where(
@@ -218,6 +235,9 @@
             pltpu.VMEM((n_freq, capacity, 2, ranks, base_here), BF16),
             pltpu.VMEM((n_freq // group, group * rows, base_here), BF16),
             pltpu.VMEM((n_freq // group, 2 * half, group * rows), BF16),
+            pltpu.VMEM((8, 2 * half), F32),
+            pltpu.VMEM((8, 2 * half), F32),
+            pltpu.VMEM((base_here, 2 * half), BF16),
             pltpu.VMEM((n_bl, 2 * ranks, 2 * half), F32),
             pltpu.SemaphoreType.DMA((CHUNKS,)),
             pltpu.SemaphoreType.DMA((CHUNKS,)),

time: 14.8 us -> 14.7 us (level)
  no operation moved by 1% of the time
where the time goes in v4:
time: 14.7 us; the launch traced here: 14.6 us
  Pallas kernels  13.9 us (95%)
  local copies, waits for them, and re-layouts  0.61 us (4%)
    pallas_call x1, Pallas kernels, local(): pl.pallas_call(functools.partial(kernel, (n_freq, n_bl, modes, half, capa...  13.9 us
    unnamed x1, local copies, waits for them, and re-layouts  0.61 us

profile of v4, /device:TPU:0, one launch (start us, length us, event | category | flops | bytes accessed | tf_op | source)
XLA Modules:
  0.0 14.6 jit_solution(13722541200358792962)
XLA Ops:
  0.0 13.9 %shard_map.55 = bf16[2,24,256]{2,1,0:T(8,128)(2,1)S(1)} custom-call(bf16[1,2,256,2048]{3,2,1,0:T(8,128)(2,1)} %vis_ref.1, bf16[2048,128]{1,0:T(8,128)(2,1)} %constant.2.clone.table_ref, s32[1,24]{1,0:T(1,128)} %bitcast.7, s32[8,24]{1,0:T(8,128)} %bitcast.6, bf16[4,8,2,4,256]{4,3,2,1,0:T(4,128)(2,1)} %factors_ref.1), custom_call_target="tpu_custom_call" | custom-call | tf_op jit(solution)/shard_map/pallas_call | solution.py:225
  14.0 0.6 %copy.7 = bf16[1,2,256,24]{2,3,1,0:T(8,128)(2,1)} copy(bf16[1,2,256,24]{2,3,1,0:T(8,128)(2,1)S(1)} %bitcast.5) | data formatting | bytes 49152

commit v5 on v4

--- a/solution.py
+++ b/solution.py
@@ -26,15 +26,6 @@
     return table.astype(BF16)
 
 
-def flip(index, bits):
-    place = 1
-    while place <= bits:
-        if bits & place:
-            index = index + place * (1 - 2 * ((index // place) % 2))
-        place *= 2
-    return index
-
-
 def kernel(
     dims, vis_ref, table_ref, owner_ref, counts_ref, factors_ref, out_ref,
     vis, table, owner, counts, held, packed, spread, slots, limits, spectrum, part,
@@ -43,28 +34,28 @@
     n_freq, n_bl, modes, half, capacity, ranks = dims
     lanes = 2 * half
     rows = capacity * 2 * ranks
-    group = min(n_freq // 2, 4)
+    group = max(2, n_freq // 32)
     deep = group * rows
     blocks = n_freq // group
+    wide = min(n_freq, 8) * rows
     base_here, step = vis.shape[2], vis.shape[3]
     me = lax.axis_index("freq")
     mine = lax.axis_index("bl")
 
-    def peers(body, chosen=None):
-        if n_freq == 8:
-            for bits in chosen or (6, 4, 7, 5, 2, 3, 1):
-                other = flip(me, bits)
-                body(bits, other, other)
-        elif chosen is None or chosen[0] == 1:
-            def turn(d, carry):
-                body(d, lax.rem(me + d, n_freq), lax.rem(me + n_freq - d, n_freq))
-                return carry
-
-            lax.fori_loop(1, n_freq, turn, 0)
+    def peers(body):
+        def turn(k, carry):
+            body(k + (k - me + n_freq) // n_freq)
+            return carry
+
+        if n_freq <= 8:
+            for k in range(n_freq - 1):
+                turn(k, 0)
+        else:
+            lax.fori_loop(0, n_freq - 1, turn, 0)
 
     barrier = pltpu.get_barrier_semaphore()
 
-    def greet(d, to, source):
+    def greet(to):
         pl.semaphore_signal(barrier, inc=1, device_id={"freq": to}, device_id_type=MESH)
 
     peers(greet)
@@ -94,10 +85,10 @@
         counts_copy.start()
         own_copy.start()
 
-    def factor_copy(d, to, at):
+    def factor_copy(to, source):
         return pltpu.make_async_remote_copy(
-            src_ref=factors_ref.at[:, to], dst_ref=held.at[at],
-            send_sem=send_sem.at[d], recv_sem=recv_sem.at[d],
+            src_ref=factors_ref.at[:, to], dst_ref=held.at[source],
+            send_sem=send_sem.at[to], recv_sem=recv_sem.at[source],
             device_id={"freq": to}, device_id_type=MESH,
         )
 
@@ -123,9 +114,9 @@
         slots[...] = jnp.broadcast_to(slot, (8, lanes))
         slot_col = jnp.broadcast_to(slot, (8, lanes)).T[:, :1]
         scale = math.sqrt(NB / ranks)
-        for g in range(blocks):
-            col = lax.broadcasted_iota(jnp.int32, (lanes, deep), 1) // (2 * ranks)
-            col = (col + g * group * capacity).astype(F32)
+        for g in range(n_freq * rows // wide):
+            col = lax.broadcasted_iota(jnp.int32, (lanes, wide), 1) // (2 * ranks)
+            col = (col + g * (wide // (2 * ranks))).astype(F32)
             spread[g] = jnp.where(slot_col == col, scale, 0.0).astype(spread.dtype)
 
         spectra = jnp.zeros((2 * base_here, lanes), F32)
@@ -148,7 +139,7 @@
         prepare()
 
     pl.semaphore_wait(barrier, n_freq - 1 + n_bl - 1)
-    peers(lambda d, to, source: factor_copy(d, to, me).start())
+    peers(lambda to: factor_copy(to, me).start())
 
     @pl.when(jnp.logical_not(leading))
     def _():
@@ -159,7 +150,7 @@
     def coefficients(block):
         from_here = pl.ds(block * group, group)
         factor = held[from_here].reshape(deep, base_here)
-        packed[block] = factor
+        packed[pl.ds(pl.multiple_of(block * deep, deep), deep)] = factor
         dense = jnp.dot(factor, spectrum[...], preferred_element_type=F32)
         row = lax.broadcasted_iota(jnp.int32, (deep, lanes), 0) // (2 * ranks)
         row = (row + block * group * capacity).astype(F32)
@@ -168,11 +159,12 @@
 
     own_copy.wait()
     total = jnp.zeros((2 * ranks, lanes), F32)
-    peers(lambda d, to, source: factor_copy(d, to, source).wait_recv(), (1, 2, 3))
     for b in range(blocks):
-        if b == 1:
-            peers(lambda d, to, source: factor_copy(d, to, source).wait_recv(), (4, 5, 6, 7))
-        total = total + coefficients(lax.rem(me // group + b, blocks))
+        block = lax.rem(me // group + b, blocks)
+        for j in range(group if b else group - 1):
+            source = block * group + (j if b else (me + 1 + j) % group)
+            factor_copy(source, source).wait_recv()
+        total = total + coefficients(block)
     rank_row = lax.broadcasted_iota(jnp.int32, (2 * ranks, lanes), 0)
     in_low = lax.broadcasted_iota(jnp.int32, (2 * ranks, lanes), 1) < half
     crossed = pltpu.roll(pltpu.roll(total, ranks, 0), half, 1)
@@ -194,21 +186,22 @@
         summed = summed + part[b]
     kept = jnp.where((rank_row % ranks).astype(F32) < limits[:2 * ranks], summed, 0.0).astype(BF16)
 
-    tiling = lax.broadcasted_iota(jnp.int32, (2 * ranks, deep), 1) % (2 * ranks)
+    tiling = lax.broadcasted_iota(jnp.int32, (2 * ranks, wide), 1) % (2 * ranks)
     tiling = jnp.where(
-        tiling == lax.broadcasted_iota(jnp.int32, (2 * ranks, deep), 0), 1.0, 0.0
+        tiling == lax.broadcasted_iota(jnp.int32, (2 * ranks, wide), 0), 1.0, 0.0
     ).astype(BF16)
     tiled = lax.dot_general(
         kept, tiling, (((0,), (0,)), ((), ())), preferred_element_type=F32
     )
     filtered = jnp.zeros((lanes, base_here), F32)
-    for g in range(blocks):
+    for g in range(n_freq * rows // wide):
         weight = (tiled * spread[g].astype(F32)).astype(BF16)
-        filtered = filtered + jnp.dot(weight, packed[g], preferred_element_type=F32)
+        factor = packed[g * wide : (g + 1) * wide]
+        filtered = filtered + jnp.dot(weight, factor, preferred_element_type=F32)
     filtered = filtered.astype(BF16)
     out_ref[0] = filtered[:modes]
     out_ref[1] = filtered[half : half + modes]
-    peers(lambda d, to, source: factor_copy(d, to, me).wait_send())
+    peers(lambda to: factor_copy(to, me).wait_send())
     for d in range(1, n_bl):
         part_copy(d, mine).wait_send()
 
@@ -219,7 +212,7 @@
     capacity, _, _, ranks, _ = factors.shape
     half = -(-2 * modes // 128) * 64
     rows = capacity * 2 * ranks
-    group = min(n_freq // 2, 4)
+    wide = min(n_freq, 8) * rows
     table = jnp.asarray(wave_table(modes, half, samples))
     stays = pl.BlockSpec(memory_space=pltpu.HBM)
     out = pl.pallas_call(
@@ -233,8 +226,8 @@
             pltpu.VMEM((1, modes), jnp.int32),
             pltpu.VMEM((n_freq, modes), jnp.int32),
             pltpu.VMEM((n_freq, capacity, 2, ranks, base_here), BF16),
-            pltpu.VMEM((n_freq // group, group * rows, base_here), BF16),
-            pltpu.VMEM((n_freq // group, 2 * half, group * rows), BF16),
+            pltpu.VMEM((n_freq * rows, base_here), BF16),
+            pltpu.VMEM((n_freq * rows // wide, 2 * half, wide), BF16),
             pltpu.VMEM((8, 2 * half), F32),
             pltpu.VMEM((8, 2 * half), F32),
             pltpu.VMEM((base_here, 2 * half), BF16),

time: 14.7 us -> 14.2 us (0.966)
  Pallas kernels: 13.9 us -> 13.4 us
    pallas_call x1, Pallas kernels: 13.9 us -> 13.4 us  [local(): pl.pallas_call(functools.partial(kernel, (n_freq, n_bl, modes, half, capa...]
where the time goes in v5:
time: 14.2 us; the launch traced here: 14.1 us
  Pallas kernels  13.4 us (94%)
  local copies, waits for them, and re-layouts  0.61 us (4%)
    pallas_call x1, Pallas kernels, local(): pl.pallas_call(functools.partial(kernel, (n_freq, n_bl, modes, half, capa...  13.4 us
    unnamed x1, local copies, waits for them, and re-layouts  0.61 us

profile of v5, /device:TPU:0, one launch (start us, length us, event | category | flops | bytes accessed | tf_op | source)
XLA Modules:
  0.0 14.1 jit_solution(10336636815780387837)
XLA Ops:
  0.0 13.4 %shard_map.55 = bf16[2,24,256]{2,1,0:T(8,128)(2,1)S(1)} custom-call(bf16[1,2,256,2048]{3,2,1,0:T(8,128)(2,1)} %vis_ref.1, bf16[2048,128]{1,0:T(8,128)(2,1)} %constant.2.clone.table_ref, s32[1,24]{1,0:T(1,128)} %bitcast.7, s32[8,24]{1,0:T(8,128)} %bitcast.6, bf16[4,8,2,4,256]{4,3,2,1,0:T(4,128)(2,1)} %factors_ref.1), custom_call_target="tpu_custom_call" | custom-call | tf_op jit(solution)/shard_map/pallas_call | solution.py:218
  13.5 0.6 %copy.7 = bf16[1,2,256,24]{2,3,1,0:T(8,128)(2,1)} copy(bf16[1,2,256,24]{2,3,1,0:T(8,128)(2,1)S(1)} %bitcast.5) | data formatting | bytes 49152

commit v6 on v5

--- a/solution.py
+++ b/solution.py
@@ -10,7 +10,7 @@
 from jax.sharding import PartitionSpec as P
 
 NB = 1024
-CHUNKS = 2
+CHUNKS = 8
 F32 = jnp.float32
 BF16 = jnp.bfloat16
 MESH = pl.DeviceIdType.MESH
@@ -28,7 +28,7 @@
 
 def kernel(
     dims, vis_ref, table_ref, owner_ref, counts_ref, factors_ref, out_ref,
-    vis, table, owner, counts, held, packed, spread, slots, limits, spectrum, part,
+    vis, table, owner, counts, held, packed, spread, slots, limits, spectra, spectrum, part,
     vis_sem, table_sem, small_sem, send_sem, recv_sem, part_send, part_recv,
 ):
     n_freq, n_bl, modes, half, capacity, ranks = dims
@@ -47,11 +47,7 @@
             body(k + (k - me + n_freq) // n_freq)
             return carry
 
-        if n_freq <= 8:
-            for k in range(n_freq - 1):
-                turn(k, 0)
-        else:
-            lax.fori_loop(0, n_freq - 1, turn, 0)
+        lax.fori_loop(0, n_freq - 1, turn, 0)
 
     barrier = pltpu.get_barrier_semaphore()
 
@@ -66,11 +62,11 @@
 
     def vis_copy(c):
         return pltpu.make_async_copy(
-            vis_ref.at[0, :, :, pl.ds(c * step, step)], vis.at[c], vis_sem.at[c]
+            vis_ref.at[0, :, :, pl.ds(pl.multiple_of(c * step, step), step)], vis.at[c], vis_sem.at[c]
         )
 
     def table_copy(c):
-        times = pl.ds(c * step, step)
+        times = pl.ds(pl.multiple_of(c * step, step), step)
         return pltpu.make_async_copy(table_ref.at[times], table.at[times], table_sem.at[c])
 
     owner_copy = pltpu.make_async_copy(owner_ref, owner, small_sem.at[0])
@@ -78,9 +74,12 @@
     own_copy = pltpu.make_async_copy(factors_ref.at[:, me], held.at[me], small_sem.at[2])
 
     def fetch():
-        for c in range(CHUNKS):
+        def begin(c, carry):
             table_copy(c).start()
             vis_copy(c).start()
+            return carry
+
+        lax.fori_loop(0, CHUNKS, begin, 0)
         owner_copy.start()
         counts_copy.start()
         own_copy.start()
@@ -119,32 +118,38 @@
             col = (col + g * (wide // (2 * ranks))).astype(F32)
             spread[g] = jnp.where(slot_col == col, scale, 0.0).astype(spread.dtype)
 
-        spectra = jnp.zeros((2 * base_here, lanes), F32)
-        for c in range(CHUNKS):
+        spectra[...] = jnp.zeros_like(spectra)
+
+        def add(c, carry):
             table_copy(c).wait()
             vis_copy(c).wait()
-            spectra = spectra + jnp.dot(
-                vis[c].reshape(2 * base_here, step), table[c * step : (c + 1) * step],
+            spectra[...] += jnp.dot(
+                vis[c].reshape(2 * base_here, step), table[pl.ds(pl.multiple_of(c * step, step), step)],
                 preferred_element_type=F32,
             )
+            return carry
+
+        lax.fori_loop(0, CHUNKS, add, 0)
         real, imag = spectra[:base_here], spectra[base_here:]
         low = lax.broadcasted_iota(jnp.int32, (base_here, lanes), 1) < half
         spectrum[...] = (jnp.where(low, real, -real) + pltpu.roll(imag, half, 1)).astype(BF16)
 
-    leading = me < n_freq // 2
-
-    @pl.when(leading)
-    def _():
-        fetch()
-        prepare()
-
-    pl.semaphore_wait(barrier, n_freq - 1 + n_bl - 1)
-    peers(lambda to: factor_copy(to, me).start())
-
-    @pl.when(jnp.logical_not(leading))
-    def _():
-        fetch()
-        prepare()
+    first_turn = (me * 2) // n_freq
+
+    def phase(turn, carry):
+        @pl.when(turn == first_turn)
+        def _():
+            fetch()
+            prepare()
+
+        @pl.when(turn != first_turn)
+        def _():
+            pl.semaphore_wait(barrier, n_freq - 1 + n_bl - 1)
+            peers(lambda to: factor_copy(to, me).start())
+
+        return carry
+
+    lax.fori_loop(0, 2, phase, 0)
 
     slot = slots[:1]
     def coefficients(block):
@@ -158,13 +163,19 @@
         return chosen.reshape(group * capacity, 2 * ranks, lanes).sum(axis=0)
 
     own_copy.wait()
-    total = jnp.zeros((2 * ranks, lanes), F32)
-    for b in range(blocks):
+
+    def arrived(b, total):
         block = lax.rem(me // group + b, blocks)
-        for j in range(group if b else group - 1):
-            source = block * group + (j if b else (me + 1 + j) % group)
-            factor_copy(source, source).wait_recv()
-        total = total + coefficients(block)
+        for j in range(group):
+            source = block * group + j
+
+            @pl.when(source != me)
+            def _():
+                factor_copy(source, source).wait_recv()
+
+        return total + coefficients(block)
+
+    total = lax.fori_loop(0, blocks, arrived, jnp.zeros((2 * ranks, lanes), F32))
     rank_row = lax.broadcasted_iota(jnp.int32, (2 * ranks, lanes), 0)
     in_low = lax.broadcasted_iota(jnp.int32, (2 * ranks, lanes), 1) < half
     crossed = pltpu.roll(pltpu.roll(total, ranks, 0), half, 1)
@@ -230,6 +241,7 @@
             pltpu.VMEM((n_freq * rows // wide, 2 * half, wide), BF16),
             pltpu.VMEM((8, 2 * half), F32),
             pltpu.VMEM((8, 2 * half), F32),
+            pltpu.VMEM((2 * base_here, 2 * half), F32),
             pltpu.VMEM((base_here, 2 * half), BF16),
             pltpu.VMEM((n_bl, 2 * ranks, 2 * half), F32),
             pltpu.SemaphoreType.DMA((CHUNKS,)),

time: 14.2 us -> 15 us (1.056)
  Pallas kernels: 13.4 us -> 14.2 us
    pallas_call x1, Pallas kernels: 13.4 us -> 14.2 us  [local(): pl.pallas_call(functools.partial(kernel, (n_freq, n_bl, modes, half, capa...]
where the time goes in v6:
time: 15 us; the launch traced here: 14.8 us
  Pallas kernels  14.2 us (95%)
  local copies, waits for them, and re-layouts  0.61 us (4%)
    pallas_call x1, Pallas kernels, local(): pl.pallas_call(functools.partial(kernel, (n_freq, n_bl, modes, half, capa...  14.2 us
    unnamed x1, local copies, waits for them, and re-layouts  0.61 us

profile of v6, /device:TPU:0, one launch (start us, length us, event | category | flops | bytes accessed | tf_op | source)
XLA Modules:
  0.0 14.8 jit_solution(17095082363353702974)
XLA Ops:
  0.0 14.2 %shard_map.55 = bf16[2,24,256]{2,1,0:T(8,128)(2,1)S(1)} custom-call(bf16[1,2,256,2048]{3,2,1,0:T(8,128)(2,1)} %vis_ref.1, bf16[2048,128]{1,0:T(8,128)(2,1)} %constant.2.clone.table_ref, s32[1,24]{1,0:T(1,128)} %bitcast.7, s32[8,24]{1,0:T(8,128)} %bitcast.6, bf16[4,8,2,4,256]{4,3,2,1,0:T(4,128)(2,1)} %factors_ref.1), custom_call_target="tpu_custom_call" | custom-call | tf_op jit(solution)/shard_map/pallas_call | solution.py:229
  14.2 0.6 %copy.7 = bf16[1,2,256,24]{2,3,1,0:T(8,128)(2,1)} copy(bf16[1,2,256,24]{2,3,1,0:T(8,128)(2,1)S(1)} %bitcast.5) | data formatting | bytes 49152

commit v7 on v5

--- a/solution.py
+++ b/solution.py
@@ -42,16 +42,25 @@
     me = lax.axis_index("freq")
     mine = lax.axis_index("bl")
 
-    def peers(body):
+    def others(count, own, body):
         def turn(k, carry):
-            body(k + (k - me + n_freq) // n_freq)
+            @pl.when(k != own)
+            def _():
+                body(k)
+
             return carry
 
-        if n_freq <= 8:
-            for k in range(n_freq - 1):
+        if count <= 8:
+            for k in range(count):
                 turn(k, 0)
         else:
-            lax.fori_loop(0, n_freq - 1, turn, 0)
+            lax.fori_loop(0, count, turn, 0)
+
+    def peers(body):
+        others(n_freq, me, body)
+
+    def partners(body):
+        others(n_bl, mine, body)
 
     barrier = pltpu.get_barrier_semaphore()
 
@@ -59,10 +68,11 @@
         pl.semaphore_signal(barrier, inc=1, device_id={"freq": to}, device_id_type=MESH)
 
     peers(greet)
-    for d in range(1, n_bl):
-        pl.semaphore_signal(
-            barrier, inc=1, device_id={"bl": lax.rem(mine + d, n_bl)}, device_id_type=MESH
-        )
+
+    def greet_partner(to):
+        pl.semaphore_signal(barrier, inc=1, device_id={"bl": to}, device_id_type=MESH)
+
+    partners(greet_partner)
 
     def vis_copy(c):
         return pltpu.make_async_copy(
@@ -148,9 +158,8 @@
 
     slot = slots[:1]
     def coefficients(block):
-        from_here = pl.ds(block * group, group)
-        factor = held[from_here].reshape(deep, base_here)
-        packed[pl.ds(pl.multiple_of(block * deep, deep), deep)] = factor
+        factor = held[block * group : (block + 1) * group].reshape(deep, base_here)
+        packed[block * deep : (block + 1) * deep] = factor
         dense = jnp.dot(factor, spectrum[...], preferred_element_type=F32)
         row = lax.broadcasted_iota(jnp.int32, (deep, lanes), 0) // (2 * ranks)
         row = (row + block * group * capacity).astype(F32)
@@ -159,28 +168,30 @@
 
     own_copy.wait()
     total = jnp.zeros((2 * ranks, lanes), F32)
-    for b in range(blocks):
-        block = lax.rem(me // group + b, blocks)
-        for j in range(group if b else group - 1):
-            source = block * group + (j if b else (me + 1 + j) % group)
-            factor_copy(source, source).wait_recv()
+    for block in range(blocks):
+        for j in range(group):
+            source = block * group + j
+
+            @pl.when(source != me)
+            def _():
+                factor_copy(source, source).wait_recv()
+
         total = total + coefficients(block)
     rank_row = lax.broadcasted_iota(jnp.int32, (2 * ranks, lanes), 0)
     in_low = lax.broadcasted_iota(jnp.int32, (2 * ranks, lanes), 1) < half
     crossed = pltpu.roll(pltpu.roll(total, ranks, 0), half, 1)
     part[mine] = total + jnp.where(in_low == (rank_row < ranks), crossed, -crossed)
 
-    def part_copy(d, at):
+    def part_copy(to, source):
         return pltpu.make_async_remote_copy(
-            src_ref=part.at[mine], dst_ref=part.at[at],
-            send_sem=part_send.at[d], recv_sem=part_recv.at[d],
-            device_id={"bl": lax.rem(mine + d, n_bl)}, device_id_type=MESH,
+            src_ref=part.at[mine], dst_ref=part.at[source],
+            send_sem=part_send.at[to], recv_sem=part_recv.at[source],
+            device_id={"bl": to}, device_id_type=MESH,
         )
 
-    for d in range(1, n_bl):
-        part_copy(d, mine).start()
-    for d in range(1, n_bl):
-        part_copy(d, lax.rem(mine + n_bl - d, n_bl)).wait_recv()
+    partners(lambda to: part_copy(to, mine).start())
+    peers(lambda to: factor_copy(to, me).wait_send())
+    partners(lambda source: part_copy(source, source).wait_recv())
     summed = part[0]
     for b in range(1, n_bl):
         summed = summed + part[b]
@@ -201,9 +212,7 @@
     filtered = filtered.astype(BF16)
     out_ref[0] = filtered[:modes]
     out_ref[1] = filtered[half : half + modes]
-    peers(lambda to: factor_copy(to, me).wait_send())
-    for d in range(1, n_bl):
-        part_copy(d, mine).wait_send()
+    partners(lambda to: part_copy(to, mine).wait_send())
 
 
 def local(n_freq, n_bl, vis_time, owner, counts, factors):

time: 14.2 us -> 14.2 us (level)
  no operation moved by 1% of the time
where the time goes in v7:
time: 14.2 us; the launch traced here: 14.1 us
  Pallas kernels  13.4 us (94%)
  local copies, waits for them, and re-layouts  0.61 us (4%)
    pallas_call x1, Pallas kernels, local(): pl.pallas_call(functools.partial(kernel, (n_freq, n_bl, modes, half, capa...  13.4 us
    unnamed x1, local copies, waits for them, and re-layouts  0.61 us

profile of v7, /device:TPU:0, one launch (start us, length us, event | category | flops | bytes accessed | tf_op | source)
XLA Modules:
  0.0 14.1 jit_solution(3302256924486831370)
XLA Ops:
  0.0 13.4 %shard_map.55 = bf16[2,24,256]{2,1,0:T(8,128)(2,1)S(1)} custom-call(bf16[1,2,256,2048]{3,2,1,0:T(8,128)(2,1)} %vis_ref.1, bf16[2048,128]{1,0:T(8,128)(2,1)} %constant.2.clone.table_ref, s32[1,24]{1,0:T(1,128)} %bitcast.7, s32[8,24]{1,0:T(8,128)} %bitcast.6, bf16[4,8,2,4,256]{4,3,2,1,0:T(4,128)(2,1)} %factors_ref.1), custom_call_target="tpu_custom_call" | custom-call | tf_op jit(solution)/shard_map/pallas_call | solution.py:227
  13.4 0.6 %copy.7 = bf16[1,2,256,24]{2,3,1,0:T(8,128)(2,1)} copy(bf16[1,2,256,24]{2,3,1,0:T(8,128)(2,1)S(1)} %bitcast.5) | data formatting | bytes 49152

commit v8 on v7

--- a/solution.py
+++ b/solution.py
@@ -42,7 +42,7 @@
     me = lax.axis_index("freq")
     mine = lax.axis_index("bl")
 
-    def others(count, own, body):
+    def others(count, own, body, order=None):
         def turn(k, carry):
             @pl.when(k != own)
             def _():
@@ -51,7 +51,7 @@
             return carry
 
         if count <= 8:
-            for k in range(count):
+            for k in order or range(count):
                 turn(k, 0)
         else:
             lax.fori_loop(0, count, turn, 0)
@@ -67,12 +67,11 @@
     def greet(to):
         pl.semaphore_signal(barrier, inc=1, device_id={"freq": to}, device_id_type=MESH)
 
-    peers(greet)
-
     def greet_partner(to):
         pl.semaphore_signal(barrier, inc=1, device_id={"bl": to}, device_id_type=MESH)
 
     partners(greet_partner)
+    others(n_freq, me, greet, range(n_freq - 1, -1, -1))
 
     def vis_copy(c):
         return pltpu.make_async_copy(
@@ -101,6 +100,9 @@
             send_sem=send_sem.at[to], recv_sem=recv_sem.at[source],
             device_id={"freq": to}, device_id_type=MESH,
         )
+
+    def used(rows_of_lanes):
+        return jnp.concatenate([rows_of_lanes[:modes], rows_of_lanes[half : half + modes]], axis=0)
 
     def prepare():
         owner_copy.wait()
@@ -122,10 +124,10 @@
         ranking = jnp.sum(before * onehot, axis=0, keepdims=True)
         slot = owner_lanes * capacity + ranking
         slots[...] = jnp.broadcast_to(slot, (8, lanes))
-        slot_col = jnp.broadcast_to(slot, (8, lanes)).T[:, :1]
+        slot_col = used(jnp.broadcast_to(slot, (8, lanes)).T)[:, :1]
         scale = math.sqrt(NB / ranks)
         for g in range(n_freq * rows // wide):
-            col = lax.broadcasted_iota(jnp.int32, (lanes, wide), 1) // (2 * ranks)
+            col = lax.broadcasted_iota(jnp.int32, (2 * modes, wide), 1) // (2 * ranks)
             col = (col + g * (wide // (2 * ranks))).astype(F32)
             spread[g] = jnp.where(slot_col == col, scale, 0.0).astype(spread.dtype)
 
@@ -201,17 +203,17 @@
     tiling = jnp.where(
         tiling == lax.broadcasted_iota(jnp.int32, (2 * ranks, wide), 0), 1.0, 0.0
     ).astype(BF16)
-    tiled = lax.dot_general(
+    tiled = used(lax.dot_general(
         kept, tiling, (((0,), (0,)), ((), ())), preferred_element_type=F32
-    )
-    filtered = jnp.zeros((lanes, base_here), F32)
+    ))
+    filtered = jnp.zeros((2 * modes, base_here), F32)
     for g in range(n_freq * rows // wide):
         weight = (tiled * spread[g].astype(F32)).astype(BF16)
         factor = packed[g * wide : (g + 1) * wide]
         filtered = filtered + jnp.dot(weight, factor, preferred_element_type=F32)
     filtered = filtered.astype(BF16)
     out_ref[0] = filtered[:modes]
-    out_ref[1] = filtered[half : half + modes]
+    out_ref[1] = filtered[modes:]
     partners(lambda to: part_copy(to, mine).wait_send())
 
 
@@ -236,7 +238,7 @@
             pltpu.VMEM((n_freq, modes), jnp.int32),
             pltpu.VMEM((n_freq, capacity, 2, ranks, base_here), BF16),
             pltpu.VMEM((n_freq * rows, base_here), BF16),
-            pltpu.VMEM((n_freq * rows // wide, 2 * half, wide), BF16),
+            pltpu.VMEM((n_freq * rows // wide, 2 * modes, wide), BF16),
             pltpu.VMEM((8, 2 * half), F32),
             pltpu.VMEM((8, 2 * half), F32),
             pltpu.VMEM((base_here, 2 * half), BF16),

time: 14.2 us -> 14.2 us (level)
  no operation moved by 1% of the time
where the time goes in v8:
time: 14.2 us; the launch traced here: 14 us
  Pallas kernels  13.4 us (94%)
  local copies, waits for them, and re-layouts  0.61 us (4%)
    pallas_call x1, Pallas kernels, local(): pl.pallas_call(functools.partial(kernel, (n_freq, n_bl, modes, half, capa...  13.4 us
    unnamed x1, local copies, waits for them, and re-layouts  0.61 us

profile of v8, /device:TPU:0, one launch (start us, length us, event | category | flops | bytes accessed | tf_op | source)
XLA Modules:
  0.0 14.0 jit_solution(17581927037703133935)
XLA Ops:
  0.0 13.4 %shard_map.55 = bf16[2,24,256]{2,1,0:T(8,128)(2,1)S(1)} custom-call(bf16[1,2,256,2048]{3,2,1,0:T(8,128)(2,1)} %vis_ref.1, bf16[2048,128]{1,0:T(8,128)(2,1)} %constant.2.clone.table_ref, s32[1,24]{1,0:T(1,128)} %bitcast.7, s32[8,24]{1,0:T(8,128)} %bitcast.6, bf16[4,8,2,4,256]{4,3,2,1,0:T(4,128)(2,1)} %factors_ref.1), custom_call_target="tpu_custom_call" | custom-call | tf_op jit(solution)/shard_map/pallas_call | solution.py:229
  13.4 0.6 %copy.7 = bf16[1,2,256,24]{2,3,1,0:T(8,128)(2,1)} copy(bf16[1,2,256,24]{2,3,1,0:T(8,128)(2,1)S(1)} %bitcast.5) | data formatting | bytes 49152

commit v9 on v7

--- a/solution.py
+++ b/solution.py
@@ -87,13 +87,15 @@
     counts_copy = pltpu.make_async_copy(counts_ref, counts, small_sem.at[1])
     own_copy = pltpu.make_async_copy(factors_ref.at[:, me], held.at[me], small_sem.at[2])
 
+    def fetch_small():
+        owner_copy.start()
+        counts_copy.start()
+        own_copy.start()
+
     def fetch():
         for c in range(CHUNKS):
             table_copy(c).start()
             vis_copy(c).start()
-        owner_copy.start()
-        counts_copy.start()
-        own_copy.start()
 
     def factor_copy(to, source):
         return pltpu.make_async_remote_copy(
@@ -146,6 +148,7 @@
     @pl.when(leading)
     def _():
         fetch()
+        fetch_small()
         prepare()
 
     pl.semaphore_wait(barrier, n_freq - 1 + n_bl - 1)
@@ -153,6 +156,9 @@
 
     @pl.when(jnp.logical_not(leading))
     def _():
+        fetch_small()
+        for k in range(n_freq // 2):
+            factor_copy(k, me).wait_send()
         fetch()
         prepare()
 
@@ -190,7 +196,11 @@
         )
 
     partners(lambda to: part_copy(to, mine).start())
-    peers(lambda to: factor_copy(to, me).wait_send())
+    for k in range(n_freq):
+        @pl.when((k != me) & (leading if k < n_freq // 2 else True))
+        def _():
+            factor_copy(k, me).wait_send()
+
     partners(lambda source: part_copy(source, source).wait_recv())
     summed = part[0]
     for b in range(1, n_bl):

time: 14.2 us -> 14.2 us (level)
  no operation moved by 1% of the time
where the time goes in v9:
time: 14.2 us; the launch traced here: 14.1 us
  Pallas kernels  13.4 us (94%)
  local copies, waits for them, and re-layouts  0.61 us (4%)
    pallas_call x1, Pallas kernels, local(): pl.pallas_call(functools.partial(kernel, (n_freq, n_bl, modes, half, capa...  13.4 us
    unnamed x1, local copies, waits for them, and re-layouts  0.61 us

profile of v9, /device:TPU:0, one launch (start us, length us, event | category | flops | bytes accessed | tf_op | source)
XLA Modules:
  0.0 14.1 jit_solution(3753835546826757648)
XLA Ops:
  0.0 13.4 %shard_map.55 = bf16[2,24,256]{2,1,0:T(8,128)(2,1)S(1)} custom-call(bf16[1,2,256,2048]{3,2,1,0:T(8,128)(2,1)} %vis_ref.1, bf16[2048,128]{1,0:T(8,128)(2,1)} %constant.2.clone.table_ref, s32[1,24]{1,0:T(1,128)} %bitcast.7, s32[8,24]{1,0:T(8,128)} %bitcast.6, bf16[4,8,2,4,256]{4,3,2,1,0:T(4,128)(2,1)} %factors_ref.1), custom_call_target="tpu_custom_call" | custom-call | tf_op jit(solution)/shard_map/pallas_call | solution.py:237
  13.4 0.6 %copy.7 = bf16[1,2,256,24]{2,3,1,0:T(8,128)(2,1)} copy(bf16[1,2,256,24]{2,3,1,0:T(8,128)(2,1)S(1)} %bitcast.5) | data formatting | bytes 49152
